TPU v7x, 128 devices: a whole 4x4x4 slice. The times are simulated.
128 devices in a mesh: rep: 16 (over x_lo, z, core), shard: 8 (over x_hi, y).
Axes of the slice: x: 4 (x_hi: 2, x_lo: 2; x = x_hi * 2 + x_lo), y: 4, z: 4, core: 2. Of those that a mesh axis runs over, the one named last changes fastest.
Arguments:
- latents: bfloat16 [16, 1024, 1024], P('rep', 'shard'), may hold values from -6 to 6
- cond: bfloat16 [16, 1024], P('rep'), may hold values from -6 to 6
- cotangent: bfloat16 [16, 1024, 1024], P('rep', 'shard'), may hold values from -6 to 6
- w_qkv: bfloat16 [1024, 3072], P('shard'), may hold values from -0.1875 to 0.1875
- bias_qv: bfloat16 [2048], P('shard'), may hold values from -3 to 3
- w_proj: bfloat16 [1024, 1024], P('shard'), may hold values from -1 to 1
- b_proj: bfloat16 [1024], P('shard'), may hold values from -3 to 3
- w_fc1: bfloat16 [1024, 4096], P('shard'), may hold values from -0.1875 to 0.1875
- b_fc1: bfloat16 [4096], P('shard'), may hold values from -3 to 3
- w_fc2: bfloat16 [4096, 1024], P('shard'), may hold values from -0.09375 to 0.09375
- b_fc2: bfloat16 [1024], P('shard'), may hold values from -3 to 3
- w_ada: bfloat16 [1024, 6144], P('shard'), may hold values from -0.1875 to 0.1875
- b_ada: bfloat16 [6144], P('shard'), may hold values from -3 to 3
Outputs:
- output: bfloat16 [16, 1024, 1024], P('rep', 'shard')
- grad_latents: bfloat16 [16, 1024, 1024], P('rep', 'shard')
- grad_cond: float32 [16, 1024], P('rep')
- grad_w_qkv: float32 [1024, 3072], P('shard')
- grad_bias_qv: float32 [2048], P('shard')
- grad_w_proj: float32 [1024, 1024], P('shard')
- grad_b_proj: float32 [1024], P('shard')
- grad_w_fc1: float32 [1024, 4096], P('shard')
- grad_b_fc1: float32 [4096], P('shard')
- grad_w_fc2: float32 [4096, 1024], P('shard')
- grad_b_fc2: float32 [1024], P('shard')
- grad_w_ada: float32 [1024, 6144], P('shard')
- grad_b_ada: float32 [6144], P('shard')
All inputs are finite; a program needn't handle non-finite values.
Results may differ from a plain program's by a relative error of at most 0.025.
Values may be sent and summed in bfloat16 or wider, within the bound.
No kernel may reach another device: no remote copies, remote signals or barrier semaphores. Data moves between devices by JAX's collectives and lax.ppermute only.
A program may use at most 192 MiB of HBM per device.

v0:
```python
import jax
import jax.numpy as jnp
from jax import lax
from jax.sharding import Mesh, PartitionSpec as P

HEAD = 64
SHARD = ("xh", "y")
CHIPS = ("xl", "z")
REP = ("xl", "z", "core")
OFFSETS = ((0, 0), (0, 1), (0, 3), (0, 2), (1, 0), (1, 1), (1, 3), (1, 2))
epsilon = 1e-06
highest = lax.Precision.HIGHEST
low = jnp.bfloat16
wide = jnp.float32


def shift(value, dx, dy):
    pairs = [(x * 4 + y, (x + dx) % 2 * 4 + (y + dy) % 4) for x in range(2) for y in range(4)]
    return lax.ppermute(value, SHARD, pairs)


def gather_turned(value):
    return [value] + [shift(value, dx, dy) for dx, dy in OFFSETS[1:]]


def scatter_turned(parts):
    total = parts[0]
    for part, (dx, dy) in zip(parts[1:], OFFSETS[1:]):
        total = total + shift(part.astype(low), dx, (4 - dy) % 4).astype(wide)
    return total


def swap_core(value):
    return lax.ppermute(value, "core", [(0, 1), (1, 0)])


def exchange(value, axes=SHARD):
    return lax.all_to_all(value, axes, 0, 0, tiled=True)


def spread(value, axes=SHARD, count=8):
    return exchange(jnp.broadcast_to(value[None], (count,) + value.shape), axes)


def normalize(values):
    centered = values - jnp.mean(values, axis=-1, keepdims=True)
    inverse = lax.rsqrt(jnp.mean(centered * centered, axis=-1, keepdims=True) + epsilon)
    return (centered * inverse, inverse)


def normalize_back(norm, inverse, grad):
    return inverse * (
        grad
        - jnp.mean(grad, axis=-1, keepdims=True)
        - norm * jnp.mean(grad * norm, axis=-1, keepdims=True)
    )


def silu(values):
    return values / (1.0 + jnp.exp(-values))


def gelu_tanh(values):
    return (
        0.5
        * values
        * (1.0 + jnp.tanh(0.7978845608028654 * (values + 0.044715 * values * values * values)))
    )


def mul(left, right):
    return lax.dot_general(left, right, (((1,), (0,)), ((), ())), preferred_element_type=wide)


def mul_t(left, right):
    return lax.dot_general(left, right, (((1,), (1,)), ((), ())), preferred_element_type=wide)


def t_mul(left, right):
    return lax.dot_general(left, right, (((0,), (0,)), ((), ())), preferred_element_type=wide)


def core_half(value, core):
    half = value.shape[0] // 2
    keep = lax.dynamic_slice_in_dim(value, core * half, half, 0)
    give = lax.dynamic_slice_in_dim(value, (1 - core) * half, half, 0).astype(low)
    return keep + swap_core(give).astype(wide)


def core_join(value, core):
    other = swap_core(value)
    first = jnp.where(core == 0, value, other)
    second = jnp.where(core == 0, other, value)
    return jnp.concatenate([first, second], axis=0)


def on_device(
    latents,
    cond,
    cotangent,
    w_qkv,
    bias_qv,
    w_proj,
    b_proj,
    w_fc1,
    b_fc1,
    w_fc2,
    b_fc2,
    w_ada,
    b_ada,
):
    stream_low = latents[0]
    upstream_low = cotangent[0]
    rows, features = stream_low.shape
    shards = 8
    own = features // shards
    units = w_fc2.shape[0]
    heads = own // HEAD
    place = lax.axis_index(SHARD)
    core = lax.axis_index("core")
    score_scale = HEAD ** (-0.5)
    cond_value = cond.astype(wide)
    cond_silu, silu_pull = jax.vjp(silu, cond_value)
    cond_low = cond_silu.astype(low)
    cond_own = lax.dynamic_slice_in_dim(cond_low, place * own, own, 1)
    mod_part = mul(cond_own, w_ada)[0]
    ada_width = w_ada.shape[1]
    blocks = jnp.arange(shards)[:, None] == place
    mod_part = mod_part + jnp.where(blocks, b_ada.astype(wide)[None, :], 0.0).reshape(ada_width)
    small = jnp.concatenate(
        [mod_part, bias_qv.astype(wide), b_proj.astype(wide), b_fc2.astype(wide)]
    )
    small_all = spread(small)
    modulation = jnp.sum(small_all[:, :ada_width], axis=0)
    shift_first, scale_first, gate_first, shift_second, scale_second, gate_second = jnp.split(
        modulation[None, :], 6, axis=1
    )
    at = ada_width
    bias_wide = small_all[:, at : at + 2 * own].reshape(1, 2 * features)
    at += 2 * own
    proj_bias = small_all[:, at : at + own].reshape(1, features)
    at += own
    second_bias = small_all[:, at : at + own].reshape(1, features)
    tokens = spread(stream_low).reshape(shards * rows, features)
    wq = exchange(
        w_qkv.reshape(own, 3, shards, own).transpose(2, 0, 1, 3).reshape(shards, own, 3 * own)
    ).reshape(features, 3 * own)
    w1 = exchange(w_fc1.reshape(own, shards, units).transpose(1, 0, 2)).reshape(features, units)
    wp = spread(w_proj).reshape(features, features)
    upstream_all = jnp.concatenate(gather_turned(upstream_low), axis=0)
    norm_first, inverse_first = normalize(tokens.astype(wide))
    attend_in = (norm_first * (1.0 + scale_first) + shift_first).astype(low)
    packed = mul(attend_in, wq)
    query_bias = lax.dynamic_slice_in_dim(bias_wide, place * own, own, 1)
    value_bias = lax.dynamic_slice_in_dim(bias_wide, features + place * own, own, 1)
    queries = (packed[:, :own] + query_bias).astype(low)
    keyset = packed[:, own : 2 * own].astype(low)
    valueset = (packed[:, 2 * own :] + value_bias).astype(low)
    length = shards * rows

    def split(value):
        return value.reshape(length, heads, HEAD)

    query_heads, key_heads, value_heads = (split(queries), split(keyset), split(valueset))
    scores = (
        jnp.einsum("qhe,khe->hqk", query_heads, key_heads, preferred_element_type=wide)
        * score_scale
    )
    row_peak = jnp.max(scores, axis=-1, keepdims=True)
    powered = jnp.exp(scores - row_peak)
    row_total = jnp.sum(powered, axis=-1, keepdims=True)
    attention = powered / row_total
    log_total = row_peak + jnp.log(row_total)
    mixed = (
        jnp.einsum("hqk,khe->qhe", attention.astype(low), value_heads, preferred_element_type=wide)
        .reshape(length, own)
        .astype(low)
    )
    mixed_tok = exchange(mixed.reshape(shards, rows, own))
    mixed_tok = mixed_tok.transpose(1, 0, 2).reshape(rows, features)
    branch = mul(mixed_tok, wp) + proj_bias
    stream = stream_low.astype(wide)
    middle = stream + gate_first * branch
    norm_second, inverse_second = normalize(middle)
    feed_in = (norm_second * (1.0 + scale_second) + shift_second).astype(low)
    feed_all = jnp.concatenate(gather_turned(feed_in), axis=0)
    hidden = mul(feed_all, w1) + b_fc1.astype(wide)[None, :]
    active_value, gelu_pull = jax.vjp(gelu_tanh, hidden)
    active = active_value.astype(low)
    branch_second_part = mul(active, w_fc2)

    def turned_parts(value):
        return [value[k * rows : (k + 1) * rows] for k in range(shards)]

    grad_branch_second = (upstream_all.astype(wide) * gate_second).astype(low)
    grad_active = mul_t(grad_branch_second, w_fc2)
    grad_hidden = gelu_pull(grad_active)[0].astype(low)
    grad_feed = scatter_turned(turned_parts(mul_t(grad_hidden, w1)))
    branch_second = scatter_turned(turned_parts(branch_second_part)) + second_bias
    output = (middle + gate_second * branch_second).astype(low)
    upstream = upstream_low.astype(wide)
    grad_gate_second = jnp.sum(upstream * branch_second, axis=0)
    grad_scale_second = jnp.sum(grad_feed * norm_second, axis=0)
    grad_shift_second = jnp.sum(grad_feed, axis=0)
    grad_middle = upstream + normalize_back(
        norm_second, inverse_second, grad_feed * (1.0 + scale_second)
    )
    grad_gate_first = jnp.sum(grad_middle * branch, axis=0)
    grad_branch = (grad_middle * gate_first).astype(low)
    grad_mixed_tok = mul_t(grad_branch, wp).astype(low)
    grad_mixed = exchange(grad_mixed_tok.reshape(rows, shards, own).transpose(1, 0, 2))
    grad_mixed = split(grad_mixed.reshape(length, own))
    again_scores = (
        jnp.einsum("qhe,khe->hqk", query_heads, key_heads, preferred_element_type=wide)
        * score_scale
    )
    again = jnp.exp(again_scores - log_total)
    grad_probs = jnp.einsum("qhe,khe->hqk", grad_mixed, value_heads, preferred_element_type=wide)
    grad_value = jnp.einsum(
        "hqk,qhe->khe", again.astype(low), grad_mixed, preferred_element_type=wide
    )
    row_delta = jnp.sum(again * grad_probs, axis=-1, keepdims=True)
    grad_scores = (again * (grad_probs - row_delta)).astype(low)
    grad_query = (
        jnp.einsum("hqk,khe->qhe", grad_scores, key_heads, preferred_element_type=wide)
        * score_scale
    )
    grad_key = (
        jnp.einsum("hqk,qhe->khe", grad_scores, query_heads, preferred_element_type=wide)
        * score_scale
    )
    grad_packed = jnp.concatenate(
        [part.reshape(length, own).astype(low) for part in (grad_query, grad_key, grad_value)],
        axis=1,
    )
    attend_part = mul_t(grad_packed, wq)
    grad_scale_first = jnp.sum(attend_part * norm_first, axis=0)
    grad_shift_first = jnp.sum(attend_part, axis=0)
    attend_sent = exchange(attend_part.astype(low).reshape(shards, rows, features))
    grad_attend = jnp.sum(attend_sent.astype(wide), axis=0)
    norm_own, inverse_own = normalize(stream)
    grad_stream = grad_middle + normalize_back(
        norm_own, inverse_own, grad_attend * (1.0 + scale_first)
    )
    grad_latents = grad_stream.astype(low)
    mod_terms = jnp.concatenate(
        [
            grad_shift_first,
            grad_scale_first,
            grad_gate_first,
            grad_shift_second,
            grad_scale_second,
            grad_gate_second,
            jnp.sum(grad_branch.astype(wide), axis=0),
        ]
    )
    mod_sums = jnp.sum(spread(mod_terms), axis=0)
    grad_modulation = mod_sums[:ada_width]
    proj_bias_term = lax.dynamic_slice_in_dim(mod_sums, ada_width + place * own, own, 0)
    cond_term = jnp.sum(w_ada.astype(wide) * grad_modulation[None, :], axis=1)
    cond_total = spread(cond_term).reshape(1, features)
    grad_cond = silu_pull(cond_total)[0]
    packed_sums = jnp.sum(grad_packed.astype(wide), axis=0)
    second_bias_sums = jnp.sum(grad_branch_second.astype(wide), axis=0)
    rep_terms = jnp.concatenate(
        [
            grad_modulation,
            cond_own[0].astype(wide),
            proj_bias_term,
            jnp.sum(grad_hidden.astype(wide), axis=0),
            lax.dynamic_slice_in_dim(second_bias_sums, place * own, own, 0),
            packed_sums,
        ]
    )
    rep_all = spread(rep_terms, REP, 16)
    grad_w_ada = lax.dot_general(
        rep_all[:, ada_width : ada_width + own],
        rep_all[:, :ada_width],
        (((0,), (0,)), ((), ())),
        precision=highest,
        preferred_element_type=wide,
    )
    rep_sums = jnp.sum(rep_all, axis=0)
    ada_own = ada_width // shards
    grad_b_ada = lax.dynamic_slice_in_dim(rep_sums, place * ada_own, ada_own, 0)
    at = ada_width + own
    grad_b_proj = rep_sums[at : at + own]
    at += own
    grad_b_fc1 = rep_sums[at : at + units]
    at += units
    grad_b_fc2 = rep_sums[at : at + own]
    at += own
    bias_all = spread(jnp.concatenate([rep_sums[at : at + own], rep_sums[at + 2 * own :]]))
    bias_all = jnp.concatenate(
        [bias_all[:, :own].reshape(features), bias_all[:, own:].reshape(features)]
    )
    grad_bias_qv = lax.dynamic_slice_in_dim(bias_all, place * 2 * own, 2 * own, 0)

    def over_rep(value):
        owned = lax.psum_scatter(value.astype(low), CHIPS, scatter_dimension=0, tiled=True)
        return core_join(lax.all_gather(owned, CHIPS, axis=0, tiled=True), core).astype(wide)

    term_second = core_half(t_mul(active, grad_branch_second), core)
    grad_w_fc2 = over_rep(term_second)
    term_first = core_half(
        t_mul(feed_all, grad_hidden)
        .reshape(shards, own, units)
        .transpose(1, 0, 2)
        .reshape(own, shards * units),
        core,
    )
    term_first = exchange(
        term_first.astype(low).reshape(own // 2, shards, units).transpose(1, 0, 2)
    )
    term_first = term_first.transpose(1, 0, 2).reshape(own // 2, shards * units)
    grad_w_fc1 = over_rep(term_first)
    term_proj = t_mul(mixed_tok, grad_branch).reshape(shards, own, features)
    term_proj = core_half(term_proj.transpose(1, 0, 2), core)
    term_proj = exchange(term_proj.astype(low).transpose(1, 0, 2))
    grad_w_proj = over_rep(jnp.sum(term_proj.astype(wide), axis=0))
    term_qkv = t_mul(attend_in, grad_packed).reshape(shards, own, 3 * own)
    term_qkv = core_half(term_qkv.transpose(1, 0, 2), core)
    term_qkv = exchange(term_qkv.astype(low).transpose(1, 0, 2))
    term_qkv = (
        term_qkv.reshape(shards, own // 2, 3, own)
        .transpose(1, 2, 0, 3)
        .reshape(own // 2, 3 * features)
    )
    grad_w_qkv = over_rep(term_qkv)
    return (
        output[None],
        grad_latents[None],
        grad_cond,
        grad_w_qkv,
        grad_bias_qv,
        grad_w_proj,
        grad_b_proj,
        grad_w_fc1,
        grad_b_fc1,
        grad_w_fc2,
        grad_b_fc2,
        grad_w_ada,
        grad_b_ada,
    )


def solution(mesh):
    fine = Mesh(mesh.devices.reshape(2, 4, 2, 2, 4), REP + SHARD)
    tokens = P(REP, SHARD, None)
    matrix = P(SHARD, None)
    vector = P(SHARD)
    params = (matrix, vector) * 5
    return jax.shard_map(
        on_device,
        mesh=fine,
        in_specs=(tokens, P(REP, None), tokens) + params,
        out_specs=(tokens, tokens, P(REP, None)) + params,
        check_vma=False,
    )
```

profile of v0, /device:TPU:0, one launch (start us, length us, event | category | flops | bytes accessed | tf_op | source)
XLA Modules:
  0.0 621.3 jit_solution(15007044505543565158)
XLA Ops:
  14.0 7.0 %all-to-all-start = ((f32[8,1,6656]{2,1,0:T(1,128)}), f32[8,1,6656]{2,1,0:T(1,128)S(1)}, u32[]{:S(2)}, u32[]{:S(2)}) async-start(f32[8,1,6656]{2,1,0:T(1,128)} %broadcast_in_dim.43), calls=%async_computation | async-start | bytes 425984 | tf_op jit(solution)/shard_map/all_to_all | solution.py:38
  23.5 6.0 all-to-all-done
  33.1 5.6 collective-permute-start.19
  48.6 8.6 %all-to-all-start.1 = ((bf16[8,128,1024]{2,1,0:T(8,128)(2,1)}), bf16[8,128,1024]{2,1,0:T(8,128)(2,1)S(1)}, u32[]{:S(2)}, u32[]{:S(2)}) async-start(bf16[8,128,1024]{2,1,0:T(8,128)(2,1)} %broadcast_in_dim.45), calls=%async_computation.1 | async-start | bytes 4194304 | tf_op jit(solution)/shard_map/all_to_all | solution.py:38
  59.9 9.9 %collective-permute-done.14 = bf16[128,1024]{1,0:T(8,128)(2,1)} collective-permute-done((bf16[128,1024]{1,0:T(8,128)(2,1)}, bf16[128,1024]{1,0:T(8,128)(2,1)}, u32[]{:S(2)}, u32[]{:S(2)}) %collective-permute-start.14) | collective-permute-done | bytes 262176 | tf_op jit(solution)/shard_map/ppermute | solution.py:19
  69.8 8.2 %collective-permute-start.17 = (bf16[128,1024]{1,0:T(8,128)(2,1)}, bf16[128,1024]{1,0:T(8,128)(2,1)S(1)}, u32[]{:S(2)}, u32[]{:S(2)}) collective-permute-start(bf16[128,1024]{1,0:T(8,128)(2,1)} %bitcast.30), channel_id=1, source_target_pairs={{0,4},{1,5},{2,6},{3,7},{4,0},{5,1},{6,2},{7,3},{8,12},{9,13},{10,... | collective-permute-start | bytes 786440 | tf_op jit(solution)/shard_map/ppermute | solution.py:19
  109.7 10.5 %all-to-all-done.4 = bf16[8,128,1024]{2,1,0:T(8,128)(2,1)} async-done(((bf16[8,128,1024]{2,1,0:T(8,128)(2,1)}), bf16[8,128,1024]{2,1,0:T(8,128)(2,1)}, u32[]{:S(2)}, u32[]{:S(2)}) %all-to-all-start.4) | async-done | bytes 2097184 | tf_op jit(solution)/shard_map/all_to_all | solution.py:38
  120.2 4.7 all-to-all-start.3
  128.3 5.5 all-to-all-done.3
  146.3 6.5 %all-to-all-done.5 = bf16[8,128,512]{1,2,0:T(8,128)(2,1)} async-done(((bf16[8,128,512]{1,2,0:T(8,128)(2,1)}), bf16[8,128,512]{1,2,0:T(8,128)(2,1)}, u32[]{:S(2)}, u32[]{:S(2)}) %all-to-all-start.5) | async-done | bytes 1048608 | tf_op jit(solution)/shard_map/all_to_all | solution.py:38
  169.0 9.7 %collective-permute-done.1 = bf16[128,1024]{1,0:T(8,128)(2,1)} collective-permute-done((bf16[128,1024]{1,0:T(8,128)(2,1)}, bf16[128,1024]{1,0:T(8,128)(2,1)}, u32[]{:S(2)}, u32[]{:S(2)}) %collective-permute-start.1) | collective-permute-done | bytes 262176 | tf_op jit(solution)/shard_map/ppermute | solution.py:19
  178.7 5.5 collective-permute-start.4
  202.9 4.6 convert_reduce_fusion.3
  219.7 4.9 collective-permute-start.13
  227.6 4.8 collective-permute-start.26
  232.3 4.6 fusion.13
  240.3 5.3 collective-permute-start.25
  293.4 4.9 all-to-all-done.6
  298.7 5.1 fusion.16
  303.8 4.6 multiply_reduce_fusion
  337.6 11.0 %all-to-all-done.14 = bf16[8,64,512]{2,1,0:T(8,128)(2,1)S(1)} async-done(((bf16[8,64,512]{2,1,0:T(8,128)(2,1)}), bf16[8,64,512]{2,1,0:T(8,128)(2,1)S(1)}, u32[]{:S(2)}, u32[]{:S(2)}) %all-to-all-start.14) | async-done | bytes 524320 | tf_op jit(solution)/shard_map/all_to_all | solution.py:38
  355.4 6.4 %all-to-all-done.10 = bf16[8,64,384]{2,1,0:T(8,128)(2,1)S(1)} async-done(((bf16[8,64,384]{2,1,0:T(8,128)(2,1)}), bf16[8,64,384]{2,1,0:T(8,128)(2,1)S(1)}, u32[]{:S(2)}, u32[]{:S(2)}) %all-to-all-start.10) | async-done | bytes 393248 | tf_op jit(solution)/shard_map/all_to_all | solution.py:38
  366.8 12.5 %all-to-all-done.13 = bf16[8,64,1024]{2,1,0:T(8,128)(2,1)S(1)} async-done(((bf16[8,64,1024]{2,1,0:T(8,128)(2,1)}), bf16[8,64,1024]{2,1,0:T(8,128)(2,1)S(1)}, u32[]{:S(2)}, u32[]{:S(2)}) %all-to-all-start.13) | async-done | bytes 1048608 | tf_op jit(solution)/shard_map/all_to_all | solution.py:38
  387.4 51.2 %all_gather.15 = bf16[256,1024]{1,0:T(8,128)(2,1)} all-gather(bf16[32,1024]{1,0:T(8,128)(2,1)} %reduce-scatter.11.cloned.1.call-done), channel_id=1, replica_groups=mesh['xl'=2,'z'=4,'core'=2,'xh'=2,'y'=4] {'xl','z'}, dimensions={0}, use_global_device_ids=true | all-gather | bytes 589824 | tf_op jit(solution)/shard_map/all_gather | solution.py:301
  439.9 30.9 %all_gather.12 = bf16[64,3072]{1,0:T(8,128)(2,1)} all-gather(bf16[8,3072]{1,0:T(8,128)(2,1)} %reduce-scatter.5.cloned.1.call-done), channel_id=1, replica_groups=mesh['xl'=2,'z'=4,'core'=2,'xh'=2,'y'=4] {'xl','z'}, dimensions={0}, use_global_device_ids=true | all-gather | bytes 442368 | tf_op jit(solution)/shard_map/all_gather | solution.py:301
  470.8 31.3 %all_gather.14 = bf16[64,4096]{1,0:T(8,128)(2,1)} all-gather(bf16[8,4096]{1,0:T(8,128)(2,1)} %reduce-scatter.9.cloned.1.call-done), channel_id=1, replica_groups=mesh['xl'=2,'z'=4,'core'=2,'xh'=2,'y'=4] {'xl','z'}, dimensions={0}, use_global_device_ids=true | all-gather | bytes 589824 | tf_op jit(solution)/shard_map/all_gather | solution.py:301
  508.9 7.6 %all-to-all-start.8 = ((f32[8,1,7168]{2,1,0:T(1,128)}), f32[8,1,7168]{2,1,0:T(1,128)S(1)}, u32[]{:S(2)}, u32[]{:S(2)}) async-start(f32[8,1,7168]{2,1,0:T(1,128)} %broadcast_in_dim.49), calls=%async_computation.8 | async-start | bytes 458752 | tf_op jit(solution)/shard_map/all_to_all | solution.py:38
  519.1 23.9 %reduce-scatter.7.cloned.1.call-done = bf16[8,1024]{1,0:T(8,128)(2,1)} async-done(((bf16[64,1024]{1,0:T(8,128)(2,1)}), bf16[8,1024]{1,0:T(8,128)(2,1)}) %reduce-scatter.7.cloned.1.call-update) | async-done | bytes 16400 | tf_op jit(solution)/shard_map/reduce_scatter | solution.py:300
  543.0 28.4 %all_gather.13 = bf16[64,1024]{1,0:T(8,128)(2,1)S(1)} all-gather(bf16[8,1024]{1,0:T(8,128)(2,1)} %reduce-scatter.7.cloned.1.call-done), channel_id=1, replica_groups=mesh['xl'=2,'z'=4,'core'=2,'xh'=2,'y'=4] {'xl','z'}, dimensions={0}, use_global_device_ids=true | all-gather | bytes 147456 | tf_op jit(solution)/shard_map/all_gather | solution.py:301
  572.7 6.4 %all-to-all-start.9 = ((f32[8,1,128]{2,1,0:T(1,128)}), f32[8,1,128]{2,1,0:T(1,128)S(1)}, u32[]{:S(2)}, u32[]{:S(2)}) async-start(f32[8,1,128]{2,1,0:T(1,128)} %broadcast_in_dim.50), calls=%async_computation.9 | async-start | bytes 8192 | tf_op jit(solution)/shard_map/all_to_all | solution.py:38
  579.3 7.4 %all-to-all-done.9 = f32[8,1,128]{2,1,0:T(1,128)S(1)} async-done(((f32[8,1,128]{2,1,0:T(1,128)}), f32[8,1,128]{2,1,0:T(1,128)S(1)}, u32[]{:S(2)}, u32[]{:S(2)}) %all-to-all-start.9) | async-done | bytes 4128 | tf_op jit(solution)/shard_map/all_to_all | solution.py:38
  595.6 6.0 all-to-all-done.11
  (333 shorter events, 256.8 us)
Async XLA Ops:
  33.1 93.5 %collective-permute-start.19 = (bf16[128,1024]{1,0:T(8,128)(2,1)}, bf16[128,1024]{1,0:T(8,128)(2,1)}, u32[]{:S(2)}, u32[]{:S(2)}) collective-permute-start(bf16[128,1024]{1,0:T(8,128)(2,1)} %bitcast.30), channel_id=1, source_target_pairs={{0,7},{1,4},{2,5},{3,6},{4,3},{5,0},{6,1},{7,2},{8,15},{9,12},{10,... | collective-permute-start | bytes 786440 | tf_op jit(solution)/shard_map/ppermute | solution.py:19
  38.6 86.3 %collective-permute-start.18 = (bf16[128,1024]{1,0:T(8,128)(2,1)}, bf16[128,1024]{1,0:T(8,128)(2,1)}, u32[]{:S(2)}, u32[]{:S(2)}) collective-permute-start(bf16[128,1024]{1,0:T(8,128)(2,1)} %bitcast.30), channel_id=1, source_target_pairs={{0,5},{1,6},{2,7},{3,4},{4,1},{5,2},{6,3},{7,0},{8,13},{9,14},{10,... | collective-permute-start | bytes 786440 | tf_op jit(solution)/shard_map/ppermute | solution.py:19
  38.6 42.8 %collective-permute-start.16 = (bf16[128,1024]{1,0:T(8,128)(2,1)}, bf16[128,1024]{1,0:T(8,128)(2,1)}, u32[]{:S(2)}, u32[]{:S(2)}) collective-permute-start(bf16[128,1024]{1,0:T(8,128)(2,1)} %bitcast.30), channel_id=1, source_target_pairs={{0,2},{1,3},{2,0},{3,1},{4,6},{5,7},{6,4},{7,5},{8,10},{9,11},{10,... | collective-permute-start | bytes 786440 | tf_op jit(solution)/shard_map/ppermute | solution.py:19
  40.9 38.8 %collective-permute-start.15 = (bf16[128,1024]{1,0:T(8,128)(2,1)}, bf16[128,1024]{1,0:T(8,128)(2,1)}, u32[]{:S(2)}, u32[]{:S(2)}) collective-permute-start(bf16[128,1024]{1,0:T(8,128)(2,1)} %bitcast.30), channel_id=1, source_target_pairs={{0,3},{1,0},{2,1},{3,2},{4,7},{5,4},{6,5},{7,6},{8,11},{9,8},{10,9... | collective-permute-start | bytes 786440 | tf_op jit(solution)/shard_map/ppermute | solution.py:19
  42.1 27.7 %collective-permute-start.14 = (bf16[128,1024]{1,0:T(8,128)(2,1)}, bf16[128,1024]{1,0:T(8,128)(2,1)}, u32[]{:S(2)}, u32[]{:S(2)}) collective-permute-start(bf16[128,1024]{1,0:T(8,128)(2,1)} %bitcast.30), channel_id=1, source_target_pairs={{0,1},{1,2},{2,3},{3,0},{4,5},{5,6},{6,7},{7,4},{8,9},{9,10},{10,1... | collective-permute-start | bytes 786440 | tf_op jit(solution)/shard_map/ppermute | solution.py:19
  48.6 41.6 %all-to-all-start.1 = ((bf16[8,128,1024]{2,1,0:T(8,128)(2,1)}), bf16[8,128,1024]{2,1,0:T(8,128)(2,1)S(1)}, u32[]{:S(2)}, u32[]{:S(2)}) async-start(bf16[8,128,1024]{2,1,0:T(8,128)(2,1)} %broadcast_in_dim.45), calls=%async_computation.1 | async-start | bytes 4194304 | tf_op jit(solution)/shard_map/all_to_all | solution.py:38
  79.7 64.9 %collective-permute-start.20 = (bf16[128,1024]{1,0:T(8,128)(2,1)}, bf16[128,1024]{1,0:T(8,128)(2,1)}, u32[]{:S(2)}, u32[]{:S(2)}) collective-permute-start(bf16[128,1024]{1,0:T(8,128)(2,1)} %bitcast.30), channel_id=1, source_target_pairs={{0,6},{1,7},{2,4},{3,5},{4,2},{5,3},{6,0},{7,1},{8,14},{9,15},{10,... | collective-permute-start | bytes 786440 | tf_op jit(solution)/shard_map/ppermute | solution.py:19
  92.7 27.4 %all-to-all-start.4 = ((bf16[8,128,1024]{2,1,0:T(8,128)(2,1)}), bf16[8,128,1024]{2,1,0:T(8,128)(2,1)}, u32[]{:S(2)}, u32[]{:S(2)}) async-start(bf16[8,128,1024]{2,1,0:T(8,128)(2,1)} %broadcast_in_dim.46), calls=%async_computation.4 | async-start | bytes 4194304 | tf_op jit(solution)/shard_map/all_to_all | solution.py:38
  142.8 23.5 %collective-permute-start = (bf16[128,1024]{1,0:T(8,128)(2,1)}, bf16[128,1024]{1,0:T(8,128)(2,1)}, u32[]{:S(2)}, u32[]{:S(2)}) collective-permute-start(bf16[128,1024]{1,0:T(8,128)(2,1)} %get-tuple-element.28), channel_id=1, source_target_pairs={{0,1},{1,2},{2,3},{3,0},{4,5},{5,6},{6,7},{7,4},{8,9},{9,10},{10,1... | collective-permute-start | bytes 786440 | tf_op jit(solution)/shard_map/ppermute | solution.py:19
  155.1 30.8 %collective-permute-start.2 = (bf16[128,1024]{1,0:T(8,128)(2,1)}, bf16[128,1024]{1,0:T(8,128)(2,1)}, u32[]{:S(2)}, u32[]{:S(2)}) collective-permute-start(bf16[128,1024]{1,0:T(8,128)(2,1)} %get-tuple-element.28), channel_id=1, source_target_pairs={{0,2},{1,3},{2,0},{3,1},{4,6},{5,7},{6,4},{7,5},{8,10},{9,11},{10,... | collective-permute-start | bytes 786440 | tf_op jit(solution)/shard_map/ppermute | solution.py:19
  157.2 21.5 %collective-permute-start.1 = (bf16[128,1024]{1,0:T(8,128)(2,1)}, bf16[128,1024]{1,0:T(8,128)(2,1)}, u32[]{:S(2)}, u32[]{:S(2)}) collective-permute-start(bf16[128,1024]{1,0:T(8,128)(2,1)} %get-tuple-element.28), channel_id=1, source_target_pairs={{0,3},{1,0},{2,1},{3,2},{4,7},{5,4},{6,5},{7,6},{8,11},{9,8},{10,9... | collective-permute-start | bytes 786440 | tf_op jit(solution)/shard_map/ppermute | solution.py:19
  158.5 35.7 %collective-permute-start.6 = (bf16[128,1024]{1,0:T(8,128)(2,1)}, bf16[128,1024]{1,0:T(8,128)(2,1)}, u32[]{:S(2)}, u32[]{:S(2)}) collective-permute-start(bf16[128,1024]{1,0:T(8,128)(2,1)} %get-tuple-element.28), channel_id=1, source_target_pairs={{0,6},{1,7},{2,4},{3,5},{4,2},{5,3},{6,0},{7,1},{8,14},{9,15},{10,... | collective-permute-start | bytes 786440 | tf_op jit(solution)/shard_map/ppermute | solution.py:19
  161.8 30.7 %collective-permute-start.5 = (bf16[128,1024]{1,0:T(8,128)(2,1)}, bf16[128,1024]{1,0:T(8,128)(2,1)}, u32[]{:S(2)}, u32[]{:S(2)}) collective-permute-start(bf16[128,1024]{1,0:T(8,128)(2,1)} %get-tuple-element.28), channel_id=1, source_target_pairs={{0,7},{1,4},{2,5},{3,6},{4,3},{5,0},{6,1},{7,2},{8,15},{9,12},{10,... | collective-permute-start | bytes 786440 | tf_op jit(solution)/shard_map/ppermute | solution.py:19
  166.2 21.3 %collective-permute-start.3 = (bf16[128,1024]{1,0:T(8,128)(2,1)}, bf16[128,1024]{1,0:T(8,128)(2,1)S(1)}, u32[]{:S(2)}, u32[]{:S(2)}) collective-permute-start(bf16[128,1024]{1,0:T(8,128)(2,1)} %get-tuple-element.28), channel_id=1, source_target_pairs={{0,4},{1,5},{2,6},{3,7},{4,0},{5,1},{6,2},{7,3},{8,12},{9,13},{10,... | collective-permute-start | bytes 786440 | tf_op jit(solution)/shard_map/ppermute | solution.py:19
  219.7 20.6 %collective-permute-start.7 = (bf16[128,1024]{1,0:T(8,128)(2,1)S(1)}, bf16[128,1024]{1,0:T(8,128)(2,1)S(1)}, u32[]{:S(2)}, u32[]{:S(2)}) collective-permute-start(bf16[128,1024]{1,0:T(8,128)(2,1)S(1)} %get-tuple-element.40), channel_id=1, source_target_pairs={{0,3},{1,0},{2,1},{3,2},{4,7},{5,4},{6,5},{7,6},{8,11},{9,8},{10,9... | collective-permute-start | bytes 786440 | tf_op jit(solution)/shard_map/ppermute | solution.py:19
  219.7 25.9 %collective-permute-start.13 = (bf16[128,1024]{1,0:T(8,128)(2,1)S(1)}, bf16[128,1024]{1,0:T(8,128)(2,1)S(1)}, u32[]{:S(2)}, u32[]{:S(2)}) collective-permute-start(bf16[128,1024]{1,0:T(8,128)(2,1)S(1)} %get-tuple-element.41), channel_id=1, source_target_pairs={{0,6},{1,7},{2,4},{3,5},{4,2},{5,3},{6,0},{7,1},{8,14},{9,15},{10,... | collective-permute-start | bytes 786440 | tf_op jit(solution)/shard_map/ppermute | solution.py:19
  225.8 21.9 %collective-permute-start.21 = (bf16[128,1024]{1,0:T(8,128)(2,1)S(1)}, bf16[128,1024]{1,0:T(8,128)(2,1)S(1)}, u32[]{:S(2)}, u32[]{:S(2)}) collective-permute-start(bf16[128,1024]{1,0:T(8,128)(2,1)S(1)} %get-tuple-element.33), channel_id=1, source_target_pairs={{0,3},{1,0},{2,1},{3,2},{4,7},{5,4},{6,5},{7,6},{8,11},{9,8},{10,9... | collective-permute-start | bytes 786440 | tf_op jit(solution)/shard_map/ppermute | solution.py:19
  227.2 20.7 %collective-permute-start.27 = (bf16[128,1024]{1,0:T(8,128)(2,1)S(1)}, bf16[128,1024]{1,0:T(8,128)(2,1)S(1)}, u32[]{:S(2)}, u32[]{:S(2)}) collective-permute-start(bf16[128,1024]{1,0:T(8,128)(2,1)S(1)} %get-tuple-element.34), channel_id=1, source_target_pairs={{0,6},{1,7},{2,4},{3,5},{4,2},{5,3},{6,0},{7,1},{8,14},{9,15},{10,... | collective-permute-start | bytes 786440 | tf_op jit(solution)/shard_map/ppermute | solution.py:19
  227.6 28.5 %collective-permute-start.26 = (bf16[128,1024]{1,0:T(8,128)(2,1)}, bf16[128,1024]{1,0:T(8,128)(2,1)}, u32[]{:S(2)}, u32[]{:S(2)}) collective-permute-start(bf16[128,1024]{1,0:T(8,128)(2,1)} %get-tuple-element.35), channel_id=1, source_target_pairs={{0,5},{1,6},{2,7},{3,4},{4,1},{5,2},{6,3},{7,0},{8,13},{9,14},{10,... | collective-permute-start | bytes 786440 | tf_op jit(solution)/shard_map/ppermute | solution.py:19
  269.3 55.2 %collective-permute-start.34 = (bf16[256,1024]{1,0:T(8,128)(2,1)}, bf16[256,1024]{1,0:T(8,128)(2,1)}, u32[]{:S(2)}, u32[]{:S(2)}) collective-permute-start(bf16[256,1024]{1,0:T(8,128)(2,1)} %dynamic-slice_convert_fusion.1), channel_id=1, source_target_pairs={{0,8},{8,0},{1,9},{9,1},{2,10},{10,2},{3,11},{11,3},{4,12},{12,4},... | collective-permute-start | bytes 1572872 | tf_op jit(solution)/shard_map/ppermute | solution.py:34
  273.9 52.8 %collective-permute-start.32 = (bf16[64,4096]{1,0:T(8,128)(2,1)}, bf16[64,4096]{1,0:T(8,128)(2,1)}, u32[]{:S(2)}, u32[]{:S(2)}) collective-permute-start(bf16[64,4096]{1,0:T(8,128)(2,1)} %copy.202), channel_id=1, source_target_pairs={{0,8},{8,0},{1,9},{9,1},{2,10},{10,2},{3,11},{11,3},{4,12},{12,4},... | collective-permute-start | bytes 1572872 | tf_op jit(solution)/shard_map/ppermute | solution.py:34
  289.2 98.2 %reduce-scatter.11.cloned.1.call-start = ((), (), s32[]{:S(2)}) async-start(), calls=%async_computation.22 | async-start | bytes 589824 | tf_op jit(solution)/shard_map/reduce_scatter | solution.py:300
  293.2 58.9 %collective-permute-start.30 = (bf16[64,8,1024]{2,0,1:T(8,128)(2,1)}, bf16[64,8,1024]{2,0,1:T(8,128)(2,1)}, u32[]{:S(2)}, u32[]{:S(2)}) collective-permute-start(bf16[64,8,1024]{2,0,1:T(8,128)(2,1)} %fusion.23), channel_id=1, source_target_pairs={{0,8},{8,0},{1,9},{9,1},{2,10},{10,2},{3,11},{11,3},{4,12},{12,4},... | collective-permute-start | bytes 3145736 | tf_op jit(solution)/shard_map/ppermute | solution.py:34
  365.3 74.6 %reduce-scatter.5.cloned.1.call-start = ((), (), s32[]{:S(2)}) async-start(), calls=%async_computation.19 | async-start | bytes 442368 | tf_op jit(solution)/shard_map/reduce_scatter | solution.py:300
  379.3 126.6 %all-to-all-start.7 = ((bf16[8,128,1024]{2,1,0:T(8,128)(2,1)}), bf16[8,128,1024]{2,1,0:T(8,128)(2,1)S(1)}, u32[]{:S(2)}, u32[]{:S(2)}) async-start(bf16[8,128,1024]{2,1,0:T(8,128)(2,1)} %bitcast.216), calls=%async_computation.7 | async-start | bytes 4194304 | tf_op jit(solution)/shard_map/all_to_all | solution.py:38
  383.0 87.8 %reduce-scatter.9.cloned.1.call-start = ((), (), s32[]{:S(2)}) async-start(), calls=%async_computation.21 | async-start | bytes 589824 | tf_op jit(solution)/shard_map/reduce_scatter | solution.py:300
  385.0 158.0 %reduce-scatter.7.cloned.1.call-start = ((), (), s32[]{:S(2)}) async-start(), calls=%async_computation.20 | async-start | bytes 147456 | tf_op jit(solution)/shard_map/reduce_scatter | solution.py:300
  438.6 63.6 %collective-permute-start.35 = (bf16[256,1024]{1,0:T(8,128)(2,1)}, bf16[256,1024]{1,0:T(8,128)(2,1)}, u32[]{:S(2)}, u32[]{:S(2)}) collective-permute-start(bf16[256,1024]{1,0:T(8,128)(2,1)} %all_gather.15), channel_id=1, source_target_pairs={{0,8},{8,0},{1,9},{9,1},{2,10},{10,2},{3,11},{11,3},{4,12},{12,4},... | collective-permute-start | bytes 1572872 | tf_op jit(solution)/shard_map/ppermute | solution.py:34
  470.8 45.6 %collective-permute-start.29 = (bf16[64,3072]{1,0:T(8,128)(2,1)}, bf16[64,3072]{1,0:T(8,128)(2,1)}, u32[]{:S(2)}, u32[]{:S(2)}) collective-permute-start(bf16[64,3072]{1,0:T(8,128)(2,1)} %all_gather.12), channel_id=1, source_target_pairs={{0,8},{8,0},{1,9},{9,1},{2,10},{10,2},{3,11},{11,3},{4,12},{12,4},... | collective-permute-start | bytes 1179656 | tf_op jit(solution)/shard_map/ppermute | solution.py:34
  502.1 89.8 %collective-permute-start.33 = (bf16[64,4096]{1,0:T(8,128)(2,1)}, bf16[64,4096]{1,0:T(8,128)(2,1)}, u32[]{:S(2)}, u32[]{:S(2)}) collective-permute-start(bf16[64,4096]{1,0:T(8,128)(2,1)} %all_gather.14), channel_id=1, source_target_pairs={{0,8},{8,0},{1,9},{9,1},{2,10},{10,2},{3,11},{11,3},{4,12},{12,4},... | collective-permute-start | bytes 1572872 | tf_op jit(solution)/shard_map/ppermute | solution.py:34
  508.9 62.6 %all-to-all-start.8 = ((f32[8,1,7168]{2,1,0:T(1,128)}), f32[8,1,7168]{2,1,0:T(1,128)S(1)}, u32[]{:S(2)}, u32[]{:S(2)}) async-start(f32[8,1,7168]{2,1,0:T(1,128)} %broadcast_in_dim.49), calls=%async_computation.8 | async-start | bytes 458752 | tf_op jit(solution)/shard_map/all_to_all | solution.py:38
  571.4 23.3 %collective-permute-start.31 = (bf16[64,1024]{1,0:T(8,128)(2,1)S(1)}, bf16[64,1024]{1,0:T(8,128)(2,1)S(1)}, u32[]{:S(2)}, u32[]{:S(2)}) collective-permute-start(bf16[64,1024]{1,0:T(8,128)(2,1)S(1)} %all_gather.13), channel_id=1, source_target_pairs={{0,8},{8,0},{1,9},{9,1},{2,10},{10,2},{3,11},{11,3},{4,12},{12,4},... | collective-permute-start | bytes 393224 | tf_op jit(solution)/shard_map/ppermute | solution.py:34
  (68 other events, 1010.4 us)
Sparse Core Ops, SparseCore 0:
  326.8 36.9 reduce-scatter.10
  368.6 41.2 reduce-scatter.4
  412.8 36.7 reduce-scatter.8
  506.0 36.9 reduce-scatter.6
where the time goes:
time: 628 us; the launch traced here: 621 us
  waiting for transfers between devices  148 us (24%)
  blocking collectives  142 us (23%)
  starting transfers between devices  138 us (22%)
  local copies, waits for them, and re-layouts  78.6 us (13%)
  matrix products  57 us (9%)
  other arithmetic  43.1 us (7%)
  between operations  15 us (2%)
    all_gather x4, blocking collectives, over_rep(): lax.all_gather(owned, CHIPS, axis=0, tiled=True)  142 us
    all_to_all x15, waiting for transfers between devices, exchange(): return lax.all_to_all(value, axes, 0, 0, tiled=True)  81.2 us
    all_to_all x15, starting transfers between devices, exchange(): return lax.all_to_all(value, axes, 0, 0, tiled=True)  71.2 us
    ppermute x28, starting transfers between devices, shift(): return lax.ppermute(value, SHARD, pairs)  65.7 us
    ppermute x28, waiting for transfers between devices, shift(): return lax.ppermute(value, SHARD, pairs)  43 us
    unnamed x123, local copies, waits for them, and re-layouts  33.5 us
    reduce_scatter x4, waiting for transfers between devices, over_rep(): lax.psum_scatter(value.astype(low), CHIPS, scatter_dimension=0, tiled=True)  24 us
    dot_general x4, matrix products, mul_t(): lax.dot_general(left, right, (((1,), (1,)), ((), ())), preferred_element_...  15.7 us
  transfers between devices with their start and end apart: 55, of which 24 were waited for; matrix products, arithmetic and copies ran while one was open for 22% of the time, Pallas kernels for 0%

commit v1 on v0

--- a/solution.py
+++ b/solution.py
@@ -298,7 +298,13 @@
 
     def over_rep(value):
         owned = lax.psum_scatter(value.astype(low), CHIPS, scatter_dimension=0, tiled=True)
-        return core_join(lax.all_gather(owned, CHIPS, axis=0, tiled=True), core).astype(wide)
+        _raise_regions = lambda axis_id, local: jnp.concatenate(
+            lax.all_to_all(
+                jnp.stack([local for _ in range(lax.axis_size(axis_id))], 0), axis_id, 0, 0
+            ),
+            0,
+        )
+        return core_join(_raise_regions(CHIPS, owned), core).astype(wide)
 
     term_second = core_half(t_mul(active, grad_branch_second), core)
     grad_w_fc2 = over_rep(term_second)

time: 628 us -> 576 us (0.917)
  blocking collectives: 142 us -> 25.7 us
  waiting for transfers between devices: 148 us -> 200 us
  starting transfers between devices: 138 us -> 147 us
    all_gather x4 -> x0, blocking collectives: 142 us -> none  [over_rep(): lax.all_gather(owned, CHIPS, axis=0, tiled=True)]
    reduce_scatter x4, waiting for transfers between devices: 24 us -> 76.8 us  [over_rep(): lax.psum_scatter(value.astype(low), CHIPS, scatter_dimension=0, tiled=True)]
    all_to_all x0 -> x2, blocking collectives: none -> 25.7 us  [the longest x1 13.5 us: exchange(): return lax.all_to_all(value, axes, 0, 0, tiled=True)]
    all_to_all x15 -> x14, waiting for transfers between devices: 81.2 us -> 68.3 us  [exchange(): return lax.all_to_all(value, axes, 0, 0, tiled=True)]
    all_to_all x0 -> x3, waiting for transfers between devices: none -> 12.9 us  [over_rep(): lax.all_to_all(jnp.stack([local for _ in range(lax.axis_size(axis_id))],...]
    all_to_all x0 -> x3, starting transfers between devices: none -> 10.5 us  [over_rep(): lax.all_to_all(jnp.stack([local for _ in range(lax.axis_size(axis_id))],...]
    unnamed x123 -> x140, local copies, waits for them, and re-layouts: 33.5 us -> 30.7 us
    all_to_all x15 -> x14, starting transfers between devices: 71.2 us -> 72.5 us  [exchange(): return lax.all_to_all(value, axes, 0, 0, tiled=True)]
  transfers between devices with their start and end apart: 55 -> 57, of which waited for: 24 -> 26; matrix products, arithmetic and copies ran while one was open for 22% -> 27% of each run, Pallas kernels for 0% -> 0%
where the time goes in v1:
time: 576 us; the launch traced here: 569 us
  waiting for transfers between devices  200 us (35%)
  starting transfers between devices  147 us (26%)
  local copies, waits for them, and re-layouts  79.4 us (14%)
  matrix products  56.1 us (10%)
  other arithmetic  44.6 us (8%)
  blocking collectives  25.7 us (4%)
  between operations  15 us (3%)
    reduce_scatter x4, waiting for transfers between devices, over_rep(): lax.psum_scatter(value.astype(low), CHIPS, scatter_dimension=0, tiled=True)  76.8 us
    all_to_all x14, starting transfers between devices, exchange(): return lax.all_to_all(value, axes, 0, 0, tiled=True)  72.5 us
    all_to_all x14, waiting for transfers between devices, exchange(): return lax.all_to_all(value, axes, 0, 0, tiled=True)  68.3 us
    ppermute x28, starting transfers between devices, shift(): return lax.ppermute(value, SHARD, pairs)  63 us
    ppermute x28, waiting for transfers between devices, shift(): return lax.ppermute(value, SHARD, pairs)  40.8 us
    unnamed x140, local copies, waits for them, and re-layouts  30.7 us
    dot_general x4, matrix products, mul_t(): lax.dot_general(left, right, (((1,), (1,)), ((), ())), preferred_element_...  15.4 us
    all_to_all x1, blocking collectives, exchange(): return lax.all_to_all(value, axes, 0, 0, tiled=True)  13.5 us
  transfers between devices with their start and end apart: 57, of which 26 were waited for; matrix products, arithmetic and copies ran while one was open for 27% of the time, Pallas kernels for 0%

profile of v1, /device:TPU:0, one launch (start us, length us, event | category | flops | bytes accessed | tf_op | source)
XLA Modules:
  0.0 568.7 jit_solution(10711178031360224973)
XLA Ops:
  14.0 7.0 %all-to-all-start = ((f32[8,1,6656]{2,1,0:T(1,128)}), f32[8,1,6656]{2,1,0:T(1,128)S(1)}, u32[]{:S(2)}, u32[]{:S(2)}) async-start(f32[8,1,6656]{2,1,0:T(1,128)} %broadcast_in_dim.43), calls=%async_computation | async-start | bytes 425984 | tf_op jit(solution)/shard_map/all_to_all | solution.py:38
  23.5 6.0 %all-to-all-done = f32[8,1,6656]{2,1,0:T(1,128)S(1)} async-done(((f32[8,1,6656]{2,1,0:T(1,128)}), f32[8,1,6656]{2,1,0:T(1,128)S(1)}, u32[]{:S(2)}, u32[]{:S(2)}) %all-to-all-start) | async-done | bytes 213024 | tf_op jit(solution)/shard_map/all_to_all | solution.py:38
  33.1 5.6 collective-permute-start.19
  48.6 8.6 %all-to-all-start.1 = ((bf16[8,128,1024]{2,1,0:T(8,128)(2,1)}), bf16[8,128,1024]{2,1,0:T(8,128)(2,1)S(1)}, u32[]{:S(2)}, u32[]{:S(2)}) async-start(bf16[8,128,1024]{2,1,0:T(8,128)(2,1)} %broadcast_in_dim.45), calls=%async_computation.1 | async-start | bytes 4194304 | tf_op jit(solution)/shard_map/all_to_all | solution.py:38
  59.9 9.9 %collective-permute-done.14 = bf16[128,1024]{1,0:T(8,128)(2,1)} collective-permute-done((bf16[128,1024]{1,0:T(8,128)(2,1)}, bf16[128,1024]{1,0:T(8,128)(2,1)}, u32[]{:S(2)}, u32[]{:S(2)}) %collective-permute-start.14) | collective-permute-done | bytes 262176 | tf_op jit(solution)/shard_map/ppermute | solution.py:19
  69.8 8.2 %collective-permute-start.17 = (bf16[128,1024]{1,0:T(8,128)(2,1)}, bf16[128,1024]{1,0:T(8,128)(2,1)S(1)}, u32[]{:S(2)}, u32[]{:S(2)}) collective-permute-start(bf16[128,1024]{1,0:T(8,128)(2,1)} %bitcast.30), channel_id=1, source_target_pairs={{0,4},{1,5},{2,6},{3,7},{4,0},{5,1},{6,2},{7,3},{8,12},{9,13},{10,... | collective-permute-start | bytes 786440 | tf_op jit(solution)/shard_map/ppermute | solution.py:19
  109.7 10.5 %all-to-all-done.4 = bf16[8,128,1024]{2,1,0:T(8,128)(2,1)} async-done(((bf16[8,128,1024]{2,1,0:T(8,128)(2,1)}), bf16[8,128,1024]{2,1,0:T(8,128)(2,1)}, u32[]{:S(2)}, u32[]{:S(2)}) %all-to-all-start.4) | async-done | bytes 2097184 | tf_op jit(solution)/shard_map/all_to_all | solution.py:38
  120.2 4.7 all-to-all-start.3
  128.3 5.5 all-to-all-done.3
  146.3 6.5 %all-to-all-done.5 = bf16[8,128,512]{1,2,0:T(8,128)(2,1)} async-done(((bf16[8,128,512]{1,2,0:T(8,128)(2,1)}), bf16[8,128,512]{1,2,0:T(8,128)(2,1)}, u32[]{:S(2)}, u32[]{:S(2)}) %all-to-all-start.5) | async-done | bytes 1048608 | tf_op jit(solution)/shard_map/all_to_all | solution.py:38
  167.2 11.4 %collective-permute-done.1 = bf16[128,1024]{1,0:T(8,128)(2,1)S(1)} collective-permute-done((bf16[128,1024]{1,0:T(8,128)(2,1)}, bf16[128,1024]{1,0:T(8,128)(2,1)S(1)}, u32[]{:S(2)}, u32[]{:S(2)}) %collective-permute-start.1) | collective-permute-done | bytes 262176 | tf_op jit(solution)/shard_map/ppermute | solution.py:19
  178.6 5.5 collective-permute-start.4
  186.2 5.5 collective-permute-done.4
  201.4 4.9 collective-permute-start.13
  206.3 5.1 convert_reduce_fusion.3
  217.5 4.8 collective-permute-start.26
  276.6 5.9 %all-to-all-done.6 = bf16[8,128,128]{2,1,0:T(8,128)(2,1)} async-done(((bf16[8,128,128]{2,1,0:T(8,128)(2,1)}), bf16[8,128,128]{2,1,0:T(8,128)(2,1)}, u32[]{:S(2)}, u32[]{:S(2)}) %all-to-all-start.6) | async-done | bytes 262176 | tf_op jit(solution)/shard_map/all_to_all | solution.py:38
  283.8 5.1 fusion.16
  321.9 11.8 %all-to-all-done.16 = bf16[8,64,512]{2,1,0:T(8,128)(2,1)S(1)} async-done(((bf16[8,64,512]{2,1,0:T(8,128)(2,1)}), bf16[8,64,512]{2,1,0:T(8,128)(2,1)S(1)}, u32[]{:S(2)}, u32[]{:S(2)}) %all-to-all-start.16) | async-done | bytes 524320 | tf_op jit(solution)/shard_map/all_to_all | solution.py:38
  333.7 13.5 %all_to_all.109 = bf16[8,64,384]{2,1,0:T(8,128)(2,1)} all-to-all(bf16[8,64,384]{2,1,0:T(8,128)(2,1)S(1)} %fusion.55), channel_id=1, replica_groups=mesh['xl'=2,'z'=4,'core'=2,'xh'=2,'y'=4] {'xh','y'}, dimensions={0} | all-to-all | bytes 786432 | tf_op jit(solution)/shard_map/all_to_all | solution.py:38
  349.7 12.2 %all_to_all.110 = bf16[8,32,1024]{2,1,0:T(8,128)(2,1)} all-to-all(bf16[8,32,1024]{2,1,0:T(8,128)(2,1)S(1)} %stack.11), channel_id=1, replica_groups=mesh['xl'=2,'z'=4,'core'=2,'xh'=2,'y'=4] {'xl','z'}, dimensions={0} | all-to-all | bytes 1048576 | tf_op jit(solution)/shard_map/all_to_all | solution.py:302
  361.9 6.2 %all-to-all-start.7 = ((bf16[8,128,1024]{2,1,0:T(8,128)(2,1)}), bf16[8,128,1024]{2,1,0:T(8,128)(2,1)S(1)}, u32[]{:S(2)}, u32[]{:S(2)}) async-start(bf16[8,128,1024]{2,1,0:T(8,128)(2,1)} %bitcast.232), calls=%async_computation.7 | async-start | bytes 4194304 | tf_op jit(solution)/shard_map/all_to_all | solution.py:38
  379.6 10.5 %all-to-all-done.7 = bf16[8,128,1024]{2,1,0:T(8,128)(2,1)S(1)} async-done(((bf16[8,128,1024]{2,1,0:T(8,128)(2,1)}), bf16[8,128,1024]{2,1,0:T(8,128)(2,1)S(1)}, u32[]{:S(2)}, u32[]{:S(2)}) %all-to-all-start.7) | async-done | bytes 2097184 | tf_op jit(solution)/shard_map/all_to_all | solution.py:38
  397.7 15.2 %reduce-scatter.7.cloned.1.call-done = bf16[8,3072]{1,0:T(8,128)(2,1)} async-done(((bf16[64,3072]{1,0:T(8,128)(2,1)}), bf16[8,3072]{1,0:T(8,128)(2,1)}) %reduce-scatter.7.cloned.1.call-update) | async-done | bytes 49168 | tf_op jit(solution)/shard_map/reduce_scatter | solution.py:300
  419.0 33.5 %reduce-scatter.13.cloned.1.call-done = bf16[8,4096]{1,0:T(8,128)(2,1)} async-done(((bf16[64,4096]{1,0:T(8,128)(2,1)}), bf16[8,4096]{1,0:T(8,128)(2,1)}) %reduce-scatter.13.cloned.1.call-update) | async-done | bytes 65552 | tf_op jit(solution)/shard_map/reduce_scatter | solution.py:300
  457.9 8.2 %all-to-all-done.17 = bf16[8,8,4096]{2,1,0:T(8,128)(2,1)S(1)} async-done(((bf16[8,8,4096]{2,1,0:T(8,128)(2,1)}), bf16[8,8,4096]{2,1,0:T(8,128)(2,1)S(1)}, u32[]{:S(2)}, u32[]{:S(2)}) %all-to-all-start.17) | async-done | bytes 524320 | tf_op jit(solution)/shard_map/all_to_all | solution.py:302
  466.9 6.4 %all-to-all-start.8 = ((f32[8,1,7168]{2,1,0:T(1,128)}), f32[8,1,7168]{2,1,0:T(1,128)}, u32[]{:S(2)}, u32[]{:S(2)}) async-start(f32[8,1,7168]{2,1,0:T(1,128)} %broadcast_in_dim.49), calls=%async_computation.8 | async-start | bytes 458752 | tf_op jit(solution)/shard_map/all_to_all | solution.py:38
  484.1 5.4 all-to-all-start.9
  490.4 26.5 %reduce-scatter.9.cloned.1.call-done = bf16[8,1024]{1,0:T(8,128)(2,1)} async-done(((bf16[64,1024]{1,0:T(8,128)(2,1)}), bf16[8,1024]{1,0:T(8,128)(2,1)}) %reduce-scatter.9.cloned.1.call-update) | async-done | bytes 16400 | tf_op jit(solution)/shard_map/reduce_scatter | solution.py:300
  523.4 4.7 all-to-all-done.15
  537.8 5.2 all-to-all-done.12
  544.5 6.4 %all-to-all-start.13 = ((f32[8,1,256]{2,1,0:T(1,128)}), f32[8,1,256]{2,1,0:T(1,128)S(1)}, u32[]{:S(2)}, u32[]{:S(2)}) async-start(f32[8,1,256]{2,1,0:T(1,128)} %broadcast_in_dim.52), calls=%async_computation.14 | async-start | bytes 16384 | tf_op jit(solution)/shard_map/all_to_all | solution.py:38
  (356 shorter events, 267.4 us)
Async XLA Ops:
  33.1 93.5 %collective-permute-start.19 = (bf16[128,1024]{1,0:T(8,128)(2,1)}, bf16[128,1024]{1,0:T(8,128)(2,1)}, u32[]{:S(2)}, u32[]{:S(2)}) collective-permute-start(bf16[128,1024]{1,0:T(8,128)(2,1)} %bitcast.30), channel_id=1, source_target_pairs={{0,7},{1,4},{2,5},{3,6},{4,3},{5,0},{6,1},{7,2},{8,15},{9,12},{10,... | collective-permute-start | bytes 786440 | tf_op jit(solution)/shard_map/ppermute | solution.py:19
  38.6 86.3 %collective-permute-start.18 = (bf16[128,1024]{1,0:T(8,128)(2,1)}, bf16[128,1024]{1,0:T(8,128)(2,1)}, u32[]{:S(2)}, u32[]{:S(2)}) collective-permute-start(bf16[128,1024]{1,0:T(8,128)(2,1)} %bitcast.30), channel_id=1, source_target_pairs={{0,5},{1,6},{2,7},{3,4},{4,1},{5,2},{6,3},{7,0},{8,13},{9,14},{10,... | collective-permute-start | bytes 786440 | tf_op jit(solution)/shard_map/ppermute | solution.py:19
  38.6 42.8 %collective-permute-start.16 = (bf16[128,1024]{1,0:T(8,128)(2,1)}, bf16[128,1024]{1,0:T(8,128)(2,1)}, u32[]{:S(2)}, u32[]{:S(2)}) collective-permute-start(bf16[128,1024]{1,0:T(8,128)(2,1)} %bitcast.30), channel_id=1, source_target_pairs={{0,2},{1,3},{2,0},{3,1},{4,6},{5,7},{6,4},{7,5},{8,10},{9,11},{10,... | collective-permute-start | bytes 786440 | tf_op jit(solution)/shard_map/ppermute | solution.py:19
  40.9 38.8 %collective-permute-start.15 = (bf16[128,1024]{1,0:T(8,128)(2,1)}, bf16[128,1024]{1,0:T(8,128)(2,1)}, u32[]{:S(2)}, u32[]{:S(2)}) collective-permute-start(bf16[128,1024]{1,0:T(8,128)(2,1)} %bitcast.30), channel_id=1, source_target_pairs={{0,3},{1,0},{2,1},{3,2},{4,7},{5,4},{6,5},{7,6},{8,11},{9,8},{10,9... | collective-permute-start | bytes 786440 | tf_op jit(solution)/shard_map/ppermute | solution.py:19
  42.1 27.7 %collective-permute-start.14 = (bf16[128,1024]{1,0:T(8,128)(2,1)}, bf16[128,1024]{1,0:T(8,128)(2,1)}, u32[]{:S(2)}, u32[]{:S(2)}) collective-permute-start(bf16[128,1024]{1,0:T(8,128)(2,1)} %bitcast.30), channel_id=1, source_target_pairs={{0,1},{1,2},{2,3},{3,0},{4,5},{5,6},{6,7},{7,4},{8,9},{9,10},{10,1... | collective-permute-start | bytes 786440 | tf_op jit(solution)/shard_map/ppermute | solution.py:19
  48.6 41.7 %all-to-all-start.1 = ((bf16[8,128,1024]{2,1,0:T(8,128)(2,1)}), bf16[8,128,1024]{2,1,0:T(8,128)(2,1)S(1)}, u32[]{:S(2)}, u32[]{:S(2)}) async-start(bf16[8,128,1024]{2,1,0:T(8,128)(2,1)} %broadcast_in_dim.45), calls=%async_computation.1 | async-start | bytes 4194304 | tf_op jit(solution)/shard_map/all_to_all | solution.py:38
  79.7 64.9 %collective-permute-start.20 = (bf16[128,1024]{1,0:T(8,128)(2,1)}, bf16[128,1024]{1,0:T(8,128)(2,1)}, u32[]{:S(2)}, u32[]{:S(2)}) collective-permute-start(bf16[128,1024]{1,0:T(8,128)(2,1)} %bitcast.30), channel_id=1, source_target_pairs={{0,6},{1,7},{2,4},{3,5},{4,2},{5,3},{6,0},{7,1},{8,14},{9,15},{10,... | collective-permute-start | bytes 786440 | tf_op jit(solution)/shard_map/ppermute | solution.py:19
  92.7 27.4 %all-to-all-start.4 = ((bf16[8,128,1024]{2,1,0:T(8,128)(2,1)}), bf16[8,128,1024]{2,1,0:T(8,128)(2,1)}, u32[]{:S(2)}, u32[]{:S(2)}) async-start(bf16[8,128,1024]{2,1,0:T(8,128)(2,1)} %broadcast_in_dim.46), calls=%async_computation.4 | async-start | bytes 4194304 | tf_op jit(solution)/shard_map/all_to_all | solution.py:38
  133.8 19.0 %all-to-all-start.5 = ((bf16[8,128,512]{1,2,0:T(8,128)(2,1)}), bf16[8,128,512]{1,2,0:T(8,128)(2,1)}, u32[]{:S(2)}, u32[]{:S(2)}) async-start(bf16[8,128,512]{1,2,0:T(8,128)(2,1)} %bitcast.221), calls=%async_computation.5 | async-start | bytes 2097152 | tf_op jit(solution)/shard_map/all_to_all | solution.py:38
  142.8 21.7 %collective-permute-start = (bf16[128,1024]{1,0:T(8,128)(2,1)}, bf16[128,1024]{1,0:T(8,128)(2,1)}, u32[]{:S(2)}, u32[]{:S(2)}) collective-permute-start(bf16[128,1024]{1,0:T(8,128)(2,1)} %get-tuple-element.28), channel_id=1, source_target_pairs={{0,1},{1,2},{2,3},{3,0},{4,5},{5,6},{6,7},{7,4},{8,9},{9,10},{10,1... | collective-permute-start | bytes 786440 | tf_op jit(solution)/shard_map/ppermute | solution.py:19
  155.1 29.7 %collective-permute-start.2 = (bf16[128,1024]{1,0:T(8,128)(2,1)}, bf16[128,1024]{1,0:T(8,128)(2,1)S(1)}, u32[]{:S(2)}, u32[]{:S(2)}) collective-permute-start(bf16[128,1024]{1,0:T(8,128)(2,1)} %get-tuple-element.28), channel_id=1, source_target_pairs={{0,2},{1,3},{2,0},{3,1},{4,6},{5,7},{6,4},{7,5},{8,10},{9,11},{10,... | collective-permute-start | bytes 786440 | tf_op jit(solution)/shard_map/ppermute | solution.py:19
  157.2 21.4 %collective-permute-start.1 = (bf16[128,1024]{1,0:T(8,128)(2,1)}, bf16[128,1024]{1,0:T(8,128)(2,1)S(1)}, u32[]{:S(2)}, u32[]{:S(2)}) collective-permute-start(bf16[128,1024]{1,0:T(8,128)(2,1)} %get-tuple-element.28), channel_id=1, source_target_pairs={{0,3},{1,0},{2,1},{3,2},{4,7},{5,4},{6,5},{7,6},{8,11},{9,8},{10,9... | collective-permute-start | bytes 786440 | tf_op jit(solution)/shard_map/ppermute | solution.py:19
  158.5 34.7 %collective-permute-start.6 = (bf16[128,1024]{1,0:T(8,128)(2,1)}, bf16[128,1024]{1,0:T(8,128)(2,1)S(1)}, u32[]{:S(2)}, u32[]{:S(2)}) collective-permute-start(bf16[128,1024]{1,0:T(8,128)(2,1)} %get-tuple-element.28), channel_id=1, source_target_pairs={{0,6},{1,7},{2,4},{3,5},{4,2},{5,3},{6,0},{7,1},{8,14},{9,15},{10,... | collective-permute-start | bytes 786440 | tf_op jit(solution)/shard_map/ppermute | solution.py:19
  161.8 30.6 %collective-permute-start.5 = (bf16[128,1024]{1,0:T(8,128)(2,1)}, bf16[128,1024]{1,0:T(8,128)(2,1)S(1)}, u32[]{:S(2)}, u32[]{:S(2)}) collective-permute-start(bf16[128,1024]{1,0:T(8,128)(2,1)} %get-tuple-element.28), channel_id=1, source_target_pairs={{0,7},{1,4},{2,5},{3,6},{4,3},{5,0},{6,1},{7,2},{8,15},{9,12},{10,... | collective-permute-start | bytes 786440 | tf_op jit(solution)/shard_map/ppermute | solution.py:19
  164.4 21.1 %collective-permute-start.3 = (bf16[128,1024]{1,0:T(8,128)(2,1)}, bf16[128,1024]{1,0:T(8,128)(2,1)S(1)}, u32[]{:S(2)}, u32[]{:S(2)}) collective-permute-start(bf16[128,1024]{1,0:T(8,128)(2,1)} %get-tuple-element.28), channel_id=1, source_target_pairs={{0,4},{1,5},{2,6},{3,7},{4,0},{5,1},{6,2},{7,3},{8,12},{9,13},{10,... | collective-permute-start | bytes 786440 | tf_op jit(solution)/shard_map/ppermute | solution.py:19
  201.4 25.4 %collective-permute-start.7 = (bf16[128,1024]{1,0:T(8,128)(2,1)S(1)}, bf16[128,1024]{1,0:T(8,128)(2,1)S(1)}, u32[]{:S(2)}, u32[]{:S(2)}) collective-permute-start(bf16[128,1024]{1,0:T(8,128)(2,1)S(1)} %get-tuple-element.40), channel_id=1, source_target_pairs={{0,3},{1,0},{2,1},{3,2},{4,7},{5,4},{6,5},{7,6},{8,11},{9,8},{10,9... | collective-permute-start | bytes 786440 | tf_op jit(solution)/shard_map/ppermute | solution.py:19
  201.4 26.4 %collective-permute-start.13 = (bf16[128,1024]{1,0:T(8,128)(2,1)S(1)}, bf16[128,1024]{1,0:T(8,128)(2,1)S(1)}, u32[]{:S(2)}, u32[]{:S(2)}) collective-permute-start(bf16[128,1024]{1,0:T(8,128)(2,1)S(1)} %get-tuple-element.41), channel_id=1, source_target_pairs={{0,6},{1,7},{2,4},{3,5},{4,2},{5,3},{6,0},{7,1},{8,14},{9,15},{10,... | collective-permute-start | bytes 786440 | tf_op jit(solution)/shard_map/ppermute | solution.py:19
  217.5 23.6 %collective-permute-start.26 = (bf16[128,1024]{1,0:T(8,128)(2,1)}, bf16[128,1024]{1,0:T(8,128)(2,1)}, u32[]{:S(2)}, u32[]{:S(2)}) collective-permute-start(bf16[128,1024]{1,0:T(8,128)(2,1)} %get-tuple-element.35), channel_id=1, source_target_pairs={{0,5},{1,6},{2,7},{3,4},{4,1},{5,2},{6,3},{7,0},{8,13},{9,14},{10,... | collective-permute-start | bytes 786440 | tf_op jit(solution)/shard_map/ppermute | solution.py:19
  227.9 18.9 %collective-permute-start.24 = (bf16[128,1024]{1,0:T(8,128)(2,1)}, bf16[128,1024]{1,0:T(8,128)(2,1)}, u32[]{:S(2)}, u32[]{:S(2)}) collective-permute-start(bf16[128,1024]{1,0:T(8,128)(2,1)} %get-tuple-element.37), channel_id=1, source_target_pairs={{0,4},{1,5},{2,6},{3,7},{4,0},{5,1},{6,2},{7,3},{8,12},{9,13},{10,... | collective-permute-start | bytes 786440 | tf_op jit(solution)/shard_map/ppermute | solution.py:19
  254.4 55.1 %collective-permute-start.34 = (bf16[256,1024]{1,0:T(8,128)(2,1)}, bf16[256,1024]{1,0:T(8,128)(2,1)}, u32[]{:S(2)}, u32[]{:S(2)}) collective-permute-start(bf16[256,1024]{1,0:T(8,128)(2,1)} %dynamic-slice_convert_fusion.1), channel_id=1, source_target_pairs={{0,8},{8,0},{1,9},{9,1},{2,10},{10,2},{3,11},{11,3},{4,12},{12,4},... | collective-permute-start | bytes 1572872 | tf_op jit(solution)/shard_map/ppermute | solution.py:34
  273.3 75.5 %reduce-scatter.11.cloned.1.call-start = ((), (), s32[]{:S(2)}) async-start(), calls=%async_computation.25 | async-start | bytes 589824 | tf_op jit(solution)/shard_map/reduce_scatter | solution.py:300
  276.5 35.3 %collective-permute-start.32 = (bf16[64,4096]{1,0:T(8,128)(2,1)}, bf16[64,4096]{1,0:T(8,128)(2,1)}, u32[]{:S(2)}, u32[]{:S(2)}) collective-permute-start(bf16[64,4096]{1,0:T(8,128)(2,1)} %copy.215), channel_id=1, source_target_pairs={{0,8},{8,0},{1,9},{9,1},{2,10},{10,2},{3,11},{11,3},{4,12},{12,4},... | collective-permute-start | bytes 1572872 | tf_op jit(solution)/shard_map/ppermute | solution.py:34
  361.9 28.2 %all-to-all-start.7 = ((bf16[8,128,1024]{2,1,0:T(8,128)(2,1)}), bf16[8,128,1024]{2,1,0:T(8,128)(2,1)S(1)}, u32[]{:S(2)}, u32[]{:S(2)}) async-start(bf16[8,128,1024]{2,1,0:T(8,128)(2,1)} %bitcast.232), calls=%async_computation.7 | async-start | bytes 4194304 | tf_op jit(solution)/shard_map/all_to_all | solution.py:38
  368.2 44.8 %reduce-scatter.7.cloned.1.call-start = ((), (), s32[]{:S(2)}) async-start(), calls=%async_computation.23 | async-start | bytes 442368 | tf_op jit(solution)/shard_map/reduce_scatter | solution.py:300
  390.1 22.8 %all-to-all-start.14 = ((bf16[8,64,1024]{2,1,0:T(8,128)(2,1)}), bf16[8,64,1024]{2,1,0:T(8,128)(2,1)}, u32[]{:S(2)}, u32[]{:S(2)}) async-start(bf16[8,64,1024]{2,1,0:T(8,128)(2,1)} %fusion.24), calls=%async_computation.15 | async-start | bytes 2097152 | tf_op jit(solution)/shard_map/all_to_all | solution.py:38
  394.4 58.2 %reduce-scatter.13.cloned.1.call-start = ((), (), s32[]{:S(2)}) async-start(), calls=%async_computation.26 | async-start | bytes 589824 | tf_op jit(solution)/shard_map/reduce_scatter | solution.py:300
  414.5 38.0 %all-to-all-start.11 = ((bf16[8,8,3072]{2,1,0:T(8,128)(2,1)}), bf16[8,8,3072]{2,1,0:T(8,128)(2,1)S(1)}, u32[]{:S(2)}, u32[]{:S(2)}) async-start(bf16[8,8,3072]{2,1,0:T(8,128)(2,1)} %stack.8), calls=%async_computation.12 | async-start | bytes 786432 | tf_op jit(solution)/shard_map/all_to_all | solution.py:302
  473.3 43.6 %reduce-scatter.9.cloned.1.call-start = ((), (), s32[]{:S(2)}) async-start(), calls=%async_computation.24 | async-start | bytes 147456 | tf_op jit(solution)/shard_map/reduce_scatter | solution.py:300
  477.3 45.0 %collective-permute-start.35 = (bf16[256,1024]{1,0:T(8,128)(2,1)S(1)}, bf16[256,1024]{1,0:T(8,128)(2,1)}, u32[]{:S(2)}, u32[]{:S(2)}) collective-permute-start(bf16[256,1024]{1,0:T(8,128)(2,1)S(1)} %bitcast.228), channel_id=1, source_target_pairs={{0,8},{8,0},{1,9},{9,1},{2,10},{10,2},{3,11},{11,3},{4,12},{12,4},... | collective-permute-start | bytes 1572872 | tf_op jit(solution)/shard_map/ppermute | solution.py:34
  479.5 56.0 %collective-permute-start.29 = (bf16[64,3072]{1,0:T(8,128)(2,1)S(1)}, bf16[64,3072]{1,0:T(8,128)(2,1)}, u32[]{:S(2)}, u32[]{:S(2)}) collective-permute-start(bf16[64,3072]{1,0:T(8,128)(2,1)S(1)} %bitcast.240), channel_id=1, source_target_pairs={{0,8},{8,0},{1,9},{9,1},{2,10},{10,2},{3,11},{11,3},{4,12},{12,4},... | collective-permute-start | bytes 1179656 | tf_op jit(solution)/shard_map/ppermute | solution.py:34
  480.1 79.2 %collective-permute-start.33 = (bf16[64,4096]{1,0:T(8,128)(2,1)S(1)}, bf16[64,4096]{1,0:T(8,128)(2,1)}, u32[]{:S(2)}, u32[]{:S(2)}) collective-permute-start(bf16[64,4096]{1,0:T(8,128)(2,1)S(1)} %bitcast.229), channel_id=1, source_target_pairs={{0,8},{8,0},{1,9},{9,1},{2,10},{10,2},{3,11},{11,3},{4,12},{12,4},... | collective-permute-start | bytes 1572872 | tf_op jit(solution)/shard_map/ppermute | solution.py:34
  484.1 32.8 %all-to-all-start.9 = ((f32[8,1,128]{2,1,0:T(1,128)}), f32[8,1,128]{2,1,0:T(1,128)S(1)}, u32[]{:S(2)}, u32[]{:S(2)}) async-start(f32[8,1,128]{2,1,0:T(1,128)} %broadcast_in_dim.50), calls=%async_computation.9 | async-start | bytes 8192 | tf_op jit(solution)/shard_map/all_to_all | solution.py:38
  (78 other events, 1129.8 us)
Sparse Core Ops, SparseCore 0:
  311.9 36.8 reduce-scatter.10
  374.9 37.9 reduce-scatter.6
  415.9 36.6 reduce-scatter.12
  479.6 37.2 reduce-scatter.8
